TPU v7x, 1024 devices: a whole 4x4x32 slice. The times are simulated.
1024 devices in a mesh: blk: 64 (over z, y_lo), grp: 16 (over x, y_hi, core).
Axes of the slice: x: 4, y: 4 (y_hi: 2, y_lo: 2; y = y_hi * 2 + y_lo), z: 32, core: 2. Of those that a mesh axis runs over, the one named last changes fastest.
Arguments:
- image: bfloat16 [49152, 1152], P(('blk', 'grp')), may hold values from -0.1796875 to 0.1796875
- text: bfloat16 [49152, 1152], P(('blk', 'grp')), may hold values from -0.1796875 to 0.1796875
- log_scale: float32 [1], replicated, may hold values from 0 to 1.1
- bias: float32 [1], replicated, may hold values from -2 to 0
Outputs:
- loss_rows: float32 [49152], P(('blk', 'grp'))
- grad_image: float32 [49152, 1152], P(('blk', 'grp'))
- grad_text: float32 [49152, 1152], P(('blk', 'grp'))
All inputs are finite; a program needn't handle non-finite values.
Results may differ from a plain program's by a relative error of at most 0.0044.
Values may be sent and summed in bfloat16 or wider, within the bound.
No kernel may reach another device: no remote copies, remote signals or barrier semaphores. Data moves between devices by JAX's collectives and lax.ppermute only.
A program may use at most 32 MiB of HBM per device.

v0:
```python
import functools

import jax
import jax.numpy as jnp
from jax import lax
from jax.experimental import pallas as pl
from jax.experimental.pallas import tpu as pltpu
from jax.sharding import PartitionSpec as P

STEPS = 8
EPS = 1e-06
PLANE = ("yl", "x", "yh")
SLOTS = 5
PACKED = 256
EXTRA = 128
PIECES = 2
LIMIT = 8 * 1024 * 1024
WHOLE = 60 * 1024 * 1024


def call(kernel, out_shape, flops=0, limit=LIMIT, **kwargs):
    return pl.pallas_call(
        kernel,
        out_shape=out_shape,
        compiler_params=pltpu.CompilerParams(vmem_limit_bytes=limit),
        cost_estimate=pl.CostEstimate(flops=flops, bytes_accessed=flops // 512, transcendentals=0) if flops else None,
        **kwargs,
    )


def along_z(value, planes, parities=(0, 1)):
    count = lax.axis_size("z")
    pairs = [(2 * z + yl, 2 * ((z + planes) % count) + yl) for z in range(count) for yl in parities]
    return lax.ppermute(value, ("z", "yl"), pairs)


def normed(rows):
    values = rows.astype(jnp.float32)
    norm = jnp.sqrt(jnp.sum(values * values, axis=-1, keepdims=True) + EPS)
    return (values / norm, norm)


def project(unit_grad, unit, norm):
    inner = jnp.sum(unit * unit_grad, axis=-1, keepdims=True)
    return (unit_grad - unit * inner) / norm


def prepare(still_hbm, moving_hbm, copies_hbm, low_hbm, still_ref, moving_ref, copy_ref, low_ref, in_sems, out_sems):
    fetches = [
        pltpu.make_async_copy(still_hbm, still_ref, in_sems.at[0]),
        pltpu.make_async_copy(moving_hbm, moving_ref, in_sems.at[1]),
    ]
    for fetch in fetches:
        fetch.start()
    fetches[0].wait()
    copy_ref[...] = normed(still_ref[...])[0].astype(jnp.bfloat16)
    rows = copy_ref.shape[0]
    stores = [
        pltpu.make_async_copy(copy_ref, copies_hbm.at[pl.ds(part * rows, rows)], out_sems.at[part])
        for part in range(copies_hbm.shape[0] // rows)
    ]
    for store in stores:
        store.start()
    fetches[1].wait()
    low_ref[...] = normed(moving_ref[...])[0].astype(jnp.bfloat16)
    stores.append(pltpu.make_async_copy(low_ref, low_hbm, in_sems.at[2]))
    stores[-1].start()
    for store in stores:
        store.wait()


def pack(*refs):
    rows, width = refs[0].shape
    for k in range(SLOTS):
        refs[-1][k * rows : (k + 1) * rows, :] = refs[k][...]
    refs[-1][SLOTS * rows :, :] = jnp.zeros((PACKED - SLOTS * rows, width), jnp.bfloat16)


def loss_lanes(loss):
    high = loss.astype(jnp.bfloat16).astype(jnp.float32)
    lane = lax.broadcasted_iota(jnp.int32, (loss.shape[0], EXTRA), 1)
    return jnp.where(lane == 0, high, jnp.where(lane == 1, loss - high, 0.0))


def score(
    rows, log_scale_ref, bias_ref, place_ref, text_hbm, own_hbm, other_hbm, grad_hbm, ours_hbm, theirs_hbm,
    text_ref, image_ref, coef_ref, grad_ref, ours_ref, theirs_ref, in_sems, out_sems,
):
    half, width = text_hbm.shape
    piece = half // PIECES
    spans = [pl.ds(part * piece, piece) for part in range(PIECES)]
    image_fetches = [
        pltpu.make_async_copy(image_hbm, image_ref.at[pl.ds(side * PACKED, PACKED)], in_sems.at[side])
        for side, image_hbm in enumerate((own_hbm, other_hbm))
    ]
    text_fetches = [
        pltpu.make_async_copy(text_hbm.at[span], text_ref.at[span], in_sems.at[2 + part])
        for part, span in enumerate(spans)
    ]
    for fetch in image_fetches + text_fetches:
        fetch.start()
    scale = jnp.exp(jnp.full((1, 1), log_scale_ref[0], jnp.float32))
    parity, place = place_ref[0], place_ref[1]
    cols = lax.broadcasted_iota(jnp.int32, (1, PACKED), 1)
    slot = jnp.zeros((1, PACKED), jnp.int32)
    for k in range(1, SLOTS):
        slot = slot + (cols >= k * rows).astype(jnp.int32)
    row_ids = lax.broadcasted_iota(jnp.int32, (piece, PACKED), 0)
    col_ids = lax.broadcasted_iota(jnp.int32, (piece, PACKED), 1)
    for fetch in image_fetches:
        fetch.wait()

    def product(part):
        text_fetches[part].wait()
        return lax.dot_general(
            text_ref[part * piece : (part + 1) * piece, :],
            image_ref[...],
            (((1,), (1,)), ((), ())),
            preferred_element_type=jnp.float32,
        )

    stores = []
    losses = [jnp.zeros((1, PACKED), jnp.float32)] * 2
    ahead = product(0)
    for part, span in enumerate(spans):
        start = part * piece
        block = start // (half // 2)
        offset = 2 * slot + block - parity
        scored = ((offset >= 0) & (offset < STEPS) & (cols < SLOTS * rows)).astype(jnp.float32)
        now = ahead
        if part + 1 < PIECES:
            ahead = product(part + 1)
        for side in range(2):
            here = slice(side * PACKED, (side + 1) * PACKED)
            logit = scale * now[:, here] + bias_ref[0]
            coef = 0.5 * jnp.tanh(0.5 * logit) + 0.5
            term = -jnp.log(1.0 - coef)
            if side == 0:
                positive = (row_ids + start == col_ids + parity * (half // 2) + place) & (col_ids < rows)
                term = term - jnp.where(positive, logit, 0.0)
                coef = coef - jnp.where(positive, 1.0, 0.0)
            losses[side] = losses[side] + scored * jnp.sum(term, axis=0, keepdims=True)
            coef_ref[start : start + piece, here] = (coef * scored).astype(jnp.bfloat16)
        grad_ref[start : start + piece, :] = jnp.dot(
            coef_ref[start : start + piece, :], image_ref[...], preferred_element_type=jnp.float32
        ).astype(jnp.bfloat16)
        stores.append(pltpu.make_async_copy(grad_ref.at[span], grad_hbm.at[span], out_sems.at[part]))
        stores[-1].start()
    for side, (out_ref, out_hbm) in reversed(list(enumerate(((ours_ref, ours_hbm), (theirs_ref, theirs_hbm))))):
        terms = lax.dot_general(
            coef_ref[:, side * PACKED : (side + 1) * PACKED],
            text_ref[...],
            (((0,), (0,)), ((), ())),
            preferred_element_type=jnp.float32,
        )
        loss = jnp.transpose(jnp.broadcast_to(losses[side], (EXTRA, PACKED)))[: SLOTS * rows, :1]
        out_ref[:, :width] = terms[: SLOTS * rows].astype(out_ref.dtype)
        out_ref[:, width:] = loss_lanes(loss).astype(out_ref.dtype)
        stores.append(pltpu.make_async_copy(out_ref, out_hbm, out_sems.at[PIECES + side]))
        stores[-1].start()
    for store in stores:
        store.wait()


def store_sum(out_ref, total):
    width = total.shape[1] - EXTRA
    out_ref[:, :width] = total[:, :width].astype(jnp.bfloat16)
    out_ref[:, width:] = loss_lanes(jnp.sum(total[:, width:], axis=1, keepdims=True)).astype(jnp.bfloat16)


def join(ours_ref, theirs_ref, *grad_refs):
    rows = grad_refs[0].shape[0]
    for k, grad_ref in enumerate(grad_refs):
        here = slice(k * rows, (k + 1) * rows)
        store_sum(grad_ref, ours_ref[here, :] + theirs_ref[here, :].astype(jnp.float32))


def sum_of(refs):
    total = refs[0][...].astype(jnp.float32)
    for ref in refs[1:]:
        total = total + ref[...].astype(jnp.float32)
    return total


def add(*refs):
    store_sum(refs[-1], sum_of(refs[:-1]))


def finish_image(count, log_scale_ref, image_ref, *refs):
    grads, (loss_ref, out_ref) = refs[:-2], refs[-2:]
    width = image_ref.shape[1]
    total = sum_of(grads)
    loss = lax.dot_general(
        jnp.full((8, EXTRA), 1.0 / count, jnp.float32),
        total[:, width:],
        (((1,), (1,)), ((), ())),
        precision=lax.Precision.HIGHEST,
        preferred_element_type=jnp.float32,
    )
    loss_ref[...] = loss[0]
    scale = jnp.exp(jnp.full((1, 1), log_scale_ref[0], jnp.float32))
    unit, norm = normed(image_ref[...])
    out_ref[...] = project(scale * total[:, :width], unit, norm)


def finish_text(log_scale_ref, text_hbm, parts_ref, grad_ref, text_ref, sem):
    fetch = pltpu.make_async_copy(text_hbm, text_ref, sem)
    fetch.start()
    rows = text_ref.shape[0]
    total = parts_ref[:rows, :].astype(jnp.float32)
    for part in range(1, parts_ref.shape[0] // rows):
        total = total + parts_ref[part * rows : (part + 1) * rows, :].astype(jnp.float32)
    scale = jnp.exp(jnp.full((1, 1), log_scale_ref[0], jnp.float32))
    fetch.wait()
    unit, norm = normed(text_ref[...])
    grad_ref[...] = project(scale * total, unit, norm)


def per_device(image, text, log_scale, bias):
    rows, width = image.shape
    plane = lax.axis_size(PLANE)
    half = rows * plane
    smem = pl.BlockSpec(memory_space=pltpu.SMEM)
    vmem = pl.BlockSpec(memory_space=pltpu.VMEM)
    hbm = pl.BlockSpec(memory_space=pltpu.HBM)
    low = jax.ShapeDtypeStruct((rows, width), jnp.bfloat16)
    wide = jax.ShapeDtypeStruct((rows, width + EXTRA), jnp.bfloat16)
    gathered = jax.ShapeDtypeStruct((half, width), jnp.bfloat16)
    full = jax.ShapeDtypeStruct((rows, width), jnp.float32)
    swap = [(0, 1), (1, 0)]
    dma = pltpu.SemaphoreType.DMA

    copies, image_low = call(
        prepare,
        (gathered, low),
        in_specs=[hbm, hbm],
        out_specs=(hbm, hbm),
        scratch_shapes=[pltpu.VMEM((rows, width), jnp.bfloat16)] * 4 + [dma((3,)), dma((plane,))],
        limit=WHOLE,
    )(text, image)
    texts = lax.all_to_all(copies, PLANE, 0, 0, tiled=True)
    one = along_z(image_low, 1)
    two = along_z(image_low, 2)
    three = along_z(two, 1)
    four = along_z(two, 2, (1,))
    own = call(pack, jax.ShapeDtypeStruct((PACKED, width), jnp.bfloat16))(image_low, one, two, three, four)
    other = lax.ppermute(own, "core", swap)

    place = jnp.stack([lax.axis_index("yl"), lax.axis_index(("x", "yh")) * rows]).astype(jnp.int32)
    packed = (SLOTS * rows, width + EXTRA)
    grads, ours, theirs = call(
        functools.partial(score, rows),
        (gathered, jax.ShapeDtypeStruct(packed, jnp.float32), jax.ShapeDtypeStruct(packed, jnp.bfloat16)),
        12 * half * PACKED * width,
        in_specs=[smem] * 3 + [hbm] * 3,
        out_specs=(hbm,) * 3,
        scratch_shapes=[
            pltpu.VMEM((half, width), jnp.bfloat16),
            pltpu.VMEM((2 * PACKED, width), jnp.bfloat16),
            pltpu.VMEM((half, 2 * PACKED), jnp.bfloat16),
            pltpu.VMEM((half, width), jnp.bfloat16),
            pltpu.VMEM(packed, jnp.float32),
            pltpu.VMEM(packed, jnp.bfloat16),
            dma((2 + PIECES,)),
            dma((2 + PIECES,)),
        ],
        limit=WHOLE,
    )(log_scale, bias, place, texts, own, other)
    parts = lax.all_to_all(grads, PLANE, 0, 0, tiled=True)
    terms = call(join, (wide,) * SLOTS)(ours, lax.ppermute(theirs, "core", swap))
    middle = call(add, wide)(terms[2], along_z(terms[3], -1), along_z(terms[4], -2, (1,)))
    back = [terms[0], along_z(terms[1], -1), along_z(middle, -2)]
    loss, grad_image = call(
        functools.partial(finish_image, float(STEPS * half)),
        (jax.ShapeDtypeStruct((rows,), jnp.float32), full),
        in_specs=[smem] + [vmem] * (1 + len(back)),
    )(log_scale, image, *back)
    grad_text = call(
        finish_text,
        full,
        in_specs=[smem, hbm, vmem],
        scratch_shapes=[pltpu.VMEM((rows, width), jnp.bfloat16), dma],
    )(log_scale, text, parts)
    return (loss, grad_image, grad_text)


def solution(mesh):
    axes = ("z", "yl", "x", "yh", "core")
    fine = jax.sharding.Mesh(mesh.devices.reshape(32, 2, 4, 2, 2), axes)
    rows = P(axes, None)
    return jax.shard_map(
        per_device,
        mesh=fine,
        in_specs=(rows, rows, P(), P()),
        out_specs=(P(axes), rows, rows),
        check_vma=False,
    )
```

profile of v0, /device:TPU:6, one launch (start us, length us, event | category | flops | bytes accessed | tf_op | source)
XLA Modules:
  0.0 97.4 jit_solution(9140709429574924239)
XLA Ops:
  0.6 2.4 %shard_map.67 = (bf16[768,1152]{1,0:T(8,128)(2,1)}, bf16[48,1152]{1,0:T(8,128)(2,1)}) custom-call(bf16[48,1152]{1,0:T(8,128)(2,1)} %text_hbm.1, bf16[48,1152]{1,0:T(8,128)(2,1)} %image_ref.1), custom_call_target="tpu_custom_call" | custom-call | tf_op jit(solution)/shard_map/pallas_call | solution.py:233
  3.1 0.0 copy-start.4
  3.1 16.8 %all-to-all-start = ((bf16[16,48,1152]{2,1,0:T(8,128)(2,1)}), bf16[16,48,1152]{2,1,0:T(8,128)(2,1)S(1)}, u32[]{:S(2)}, u32[]{:S(2)}) async-start(bf16[16,48,1152]{2,1,0:T(8,128)(2,1)} %bitcast.8), calls=%async_computation | async-start | bytes 3538944 | tf_op jit(solution)/shard_map/all_to_all | solution.py:241
  19.9 0.0 copy-done.4
  19.9 1.9 %collective-permute-start.1 = (bf16[48,1152]{1,0:T(8,128)(2,1)S(1)}, bf16[48,1152]{1,0:T(8,128)(2,1)S(1)}, u32[]{:S(2)}, u32[]{:S(2)}) collective-permute-start(bf16[48,1152]{1,0:T(8,128)(2,1)S(1)} %copy-done.4), channel_id=1, source_target_pairs={{0,64},{16,80},{32,96},{48,112},{64,128},{80,144},{96,160},{112,17... | collective-permute-start | bytes 331784 | tf_op jit(solution)/shard_map/ppermute | solution.py:34
  21.8 1.9 %collective-permute-start = (bf16[48,1152]{1,0:T(8,128)(2,1)S(1)}, bf16[48,1152]{1,0:T(8,128)(2,1)S(1)}, u32[]{:S(2)}, u32[]{:S(2)}) collective-permute-start(bf16[48,1152]{1,0:T(8,128)(2,1)S(1)} %copy-done.4), channel_id=1, source_target_pairs={{0,32},{16,48},{32,64},{48,80},{64,96},{80,112},{96,128},{112,144}... | collective-permute-start | bytes 331784 | tf_op jit(solution)/shard_map/ppermute | solution.py:34
  23.7 10.8 %collective-permute-done.1.refs_2_ = bf16[48,1152]{1,0:T(8,128)(2,1)S(1)} collective-permute-done((bf16[48,1152]{1,0:T(8,128)(2,1)S(1)}, bf16[48,1152]{1,0:T(8,128)(2,1)S(1)}, u32[]{:S(2)}, u32[]{:S(2)}) %collective-permute-start.1) | collective-permute-done | bytes 110624 | tf_op jit(solution)/shard_map/ppermute | solution.py:34
  34.5 0.7 collective-permute-start.3
  35.2 3.6 %collective-permute-start.2 = (bf16[48,1152]{1,0:T(8,128)(2,1)S(1)}, bf16[48,1152]{1,0:T(8,128)(2,1)S(1)}, u32[]{:S(2)}, u32[]{:S(2)}) collective-permute-start(bf16[48,1152]{1,0:T(8,128)(2,1)S(1)} %collective-permute-done.1.refs_2_), channel_id=1, source_target_pairs={{0,32},{16,48},{32,64},{48,80},{64,96},{80,112},{96,128},{112,144}... | collective-permute-start | bytes 331784 | tf_op jit(solution)/shard_map/ppermute | solution.py:34
  38.8 0.0 collective-permute-done.refs_1_
  38.8 0.0 collective-permute-done.3.refs_4_
  38.8 4.2 %collective-permute-done.2.refs_3_ = bf16[48,1152]{1,0:T(8,128)(2,1)S(1)} collective-permute-done((bf16[48,1152]{1,0:T(8,128)(2,1)S(1)}, bf16[48,1152]{1,0:T(8,128)(2,1)S(1)}, u32[]{:S(2)}, u32[]{:S(2)}) %collective-permute-start.2) | collective-permute-done | bytes 110624 | tf_op jit(solution)/shard_map/ppermute | solution.py:34
  43.1 0.0 copy-start.1
  43.1 1.9 %collective-permute-start.4 = (bf16[256,1152]{1,0:T(8,128)(2,1)S(1)}, bf16[256,1152]{1,0:T(8,128)(2,1)S(1)}, u32[]{:S(2)}, u32[]{:S(2)}) collective-permute-start(bf16[256,1152]{1,0:T(8,128)(2,1)S(1)} %shard_map.68.own_hbm), channel_id=1, source_target_pairs={{0,1},{1,0},{2,3},{3,2},{4,5},{5,4},{6,7},{7,6},{8,9},{9,8},{10,11... | collective-permute-start | bytes 1769480 | tf_op jit(solution)/shard_map/ppermute | solution.py:247
  46.3 0.6 pad_add_fusion.place_ref
  46.9 0.1 collective-permute-done.4.other_hbm
  47.0 0.0 copy-start.6
  47.0 0.0 all-to-all-done
  47.0 0.0 copy-start.5
  47.0 0.0 copy-done.1
  47.0 0.8 copy-done.6
  47.8 0.6 copy-done.5
  48.4 7.4 %shard_map.69 = (bf16[768,1152]{1,0:T(8,128)(2,1)}, f32[240,1280]{1,0:T(8,128)}, bf16[240,1280]{1,0:T(8,128)(2,1)}) custom-call(f32[1]{0:T(128)S(6)} %copy.7.log_scale_ref, f32[1]{0:T(128)S(6)} %copy.8.bias_ref, s32[2]{0:T(128)} %pad_add_fusion.place_ref, bf16[768,1152]{1,0:T(8,128)(2,1)} %bitcast.7, bf16[256,1152]{1,0:T(8,128)(2,1)} %copy-done.1, ...), custom_call_target="tpu_custom_call" | custom-call | flops 2717908992 | bytes 5308416 | tf_op jit(solution)/shard_map/pallas_call | solution.py:251
  55.7 0.0 copy-start
  55.7 10.9 %all-to-all-start.1 = ((bf16[16,48,1152]{2,1,0:T(8,128)(2,1)}), bf16[16,48,1152]{2,1,0:T(8,128)(2,1)S(1)}, u32[]{:S(2)}, u32[]{:S(2)}) async-start(bf16[16,48,1152]{2,1,0:T(8,128)(2,1)} %bitcast.9), calls=%async_computation.1 | async-start | bytes 3538944 | tf_op jit(solution)/shard_map/all_to_all | solution.py:269
  66.6 0.0 copy-start.2
  66.6 0.0 copy-start.3
  66.6 2.1 %collective-permute-start.5 = (bf16[240,1280]{1,0:T(8,128)(2,1)}, bf16[240,1280]{1,0:T(8,128)(2,1)S(1)}, u32[]{:S(2)}, u32[]{:S(2)}) collective-permute-start(bf16[240,1280]{1,0:T(8,128)(2,1)} %get-tuple-element.18), channel_id=1, source_target_pairs={{0,1},{1,0},{2,3},{3,2},{4,5},{5,4},{6,7},{7,6},{8,9},{9,8},{10,11... | collective-permute-start | bytes 1843208 | tf_op jit(solution)/shard_map/ppermute | solution.py:270
  68.7 2.2 %collective-permute-done.5.theirs_ref = bf16[240,1280]{1,0:T(8,128)(2,1)S(1)} collective-permute-done((bf16[240,1280]{1,0:T(8,128)(2,1)}, bf16[240,1280]{1,0:T(8,128)(2,1)S(1)}, u32[]{:S(2)}, u32[]{:S(2)}) %collective-permute-start.5) | collective-permute-done | bytes 614432 | tf_op jit(solution)/shard_map/ppermute | solution.py:270
  70.9 0.0 copy-done
  70.9 0.2 shard_map.70
  71.1 5.0 %collective-permute-start.7 = (bf16[48,1280]{1,0:T(8,128)(2,1)S(1)}, bf16[48,1280]{1,0:T(8,128)(2,1)S(1)}, u32[]{:S(2)}, u32[]{:S(2)}) collective-permute-start(bf16[48,1280]{1,0:T(8,128)(2,1)S(1)} %get-tuple-element.22), channel_id=1, source_target_pairs={{0,992},{16,1008},{32,0},{48,16},{64,32},{80,48},{96,64},{112,80},... | collective-permute-start | bytes 368648 | tf_op jit(solution)/shard_map/ppermute | solution.py:34
  76.1 0.7 collective-permute-start.8
  76.8 2.9 %collective-permute-start.6 = (bf16[48,1280]{1,0:T(8,128)(2,1)S(1)}, bf16[48,1280]{1,0:T(8,128)(2,1)S(1)}, u32[]{:S(2)}, u32[]{:S(2)}) collective-permute-start(bf16[48,1280]{1,0:T(8,128)(2,1)S(1)} %get-tuple-element.20), channel_id=1, source_target_pairs={{0,992},{16,1008},{32,0},{48,16},{64,32},{80,48},{96,64},{112,80},... | collective-permute-start | bytes 368648 | tf_op jit(solution)/shard_map/ppermute | solution.py:34
  79.7 0.0 collective-permute-done.7.refs_1_
  79.7 0.0 collective-permute-done.8.refs_2_
  79.7 0.1 shard_map.71
  79.8 4.1 %collective-permute-start.9 = (bf16[48,1280]{1,0:T(8,128)(2,1)S(1)}, bf16[48,1280]{1,0:T(8,128)(2,1)S(1)}, u32[]{:S(2)}, u32[]{:S(2)}) collective-permute-start(bf16[48,1280]{1,0:T(8,128)(2,1)S(1)} %shard_map.71), channel_id=1, source_target_pairs={{0,960},{16,976},{32,992},{48,1008},{64,0},{80,16},{96,32},{112,48... | collective-permute-start | bytes 368648 | tf_op jit(solution)/shard_map/ppermute | solution.py:34
  83.9 0.0 collective-permute-done.6.refs_1_
  83.9 5.5 %collective-permute-done.9.refs_2_ = bf16[48,1280]{1,0:T(8,128)(2,1)S(1)} collective-permute-done((bf16[48,1280]{1,0:T(8,128)(2,1)S(1)}, bf16[48,1280]{1,0:T(8,128)(2,1)S(1)}, u32[]{:S(2)}, u32[]{:S(2)}) %collective-permute-start.9) | collective-permute-done | bytes 122912 | tf_op jit(solution)/shard_map/ppermute | solution.py:34
  89.4 0.0 copy-done.2
  89.4 0.9 shard_map.72
  90.3 5.7 %all-to-all-done.1 = bf16[16,48,1152]{2,1,0:T(8,128)(2,1)S(1)} async-done(((bf16[16,48,1152]{2,1,0:T(8,128)(2,1)}), bf16[16,48,1152]{2,1,0:T(8,128)(2,1)S(1)}, u32[]{:S(2)}, u32[]{:S(2)}) %all-to-all-start.1) | async-done | bytes 1769504 | tf_op jit(solution)/shard_map/all_to_all | solution.py:269
  96.0 0.0 copy-done.3
  96.0 1.4 %shard_map.73 = f32[48,1152]{1,0:T(8,128)} custom-call(f32[1]{0:T(128)S(6)} %copy.7.log_scale_ref, bf16[48,1152]{1,0:T(8,128)(2,1)S(1)} %copy-done.3, bf16[768,1152]{1,0:T(8,128)(2,1)S(1)} %bitcast.6), custom_call_target="tpu_custom_call" | custom-call | tf_op jit(solution)/shard_map/pallas_call | solution.py:278
  (1 shorter events, 0.0 us)
Async XLA Ops:
  3.1 16.8 %copy-start.4 = (bf16[48,1152]{1,0:T(8,128)(2,1)S(1)}, bf16[48,1152]{1,0:T(8,128)(2,1)}, u32[]{:S(2)}) copy-start(bf16[48,1152]{1,0:T(8,128)(2,1)} %get-tuple-element.16.refs_0_) | copy-start | bytes 331780
  3.1 43.9 %all-to-all-start = ((bf16[16,48,1152]{2,1,0:T(8,128)(2,1)}), bf16[16,48,1152]{2,1,0:T(8,128)(2,1)S(1)}, u32[]{:S(2)}, u32[]{:S(2)}) async-start(bf16[16,48,1152]{2,1,0:T(8,128)(2,1)} %bitcast.8), calls=%async_computation | async-start | bytes 3538944 | tf_op jit(solution)/shard_map/all_to_all | solution.py:241
  19.9 14.6 %collective-permute-start.1 = (bf16[48,1152]{1,0:T(8,128)(2,1)S(1)}, bf16[48,1152]{1,0:T(8,128)(2,1)S(1)}, u32[]{:S(2)}, u32[]{:S(2)}) collective-permute-start(bf16[48,1152]{1,0:T(8,128)(2,1)S(1)} %copy-done.4), channel_id=1, source_target_pairs={{0,64},{16,80},{32,96},{48,112},{64,128},{80,144},{96,160},{112,17... | collective-permute-start | bytes 331784 | tf_op jit(solution)/shard_map/ppermute | solution.py:34
  21.8 17.0 %collective-permute-start = (bf16[48,1152]{1,0:T(8,128)(2,1)S(1)}, bf16[48,1152]{1,0:T(8,128)(2,1)S(1)}, u32[]{:S(2)}, u32[]{:S(2)}) collective-permute-start(bf16[48,1152]{1,0:T(8,128)(2,1)S(1)} %copy-done.4), channel_id=1, source_target_pairs={{0,32},{16,48},{32,64},{48,80},{64,96},{80,112},{96,128},{112,144}... | collective-permute-start | bytes 331784 | tf_op jit(solution)/shard_map/ppermute | solution.py:34
  34.5 4.3 %collective-permute-start.3 = (bf16[48,1152]{1,0:T(8,128)(2,1)S(1)}, bf16[48,1152]{1,0:T(8,128)(2,1)S(1)}, u32[]{:S(2)}, u32[]{:S(2)}) collective-permute-start(bf16[48,1152]{1,0:T(8,128)(2,1)S(1)} %collective-permute-done.1.refs_2_), channel_id=1, source_target_pairs={{16,80},{48,112},{80,144},{112,176},{144,208},{176,240},{208,272},... | collective-permute-start | bytes 331784 | tf_op jit(solution)/shard_map/ppermute | solution.py:34
  35.2 7.9 %collective-permute-start.2 = (bf16[48,1152]{1,0:T(8,128)(2,1)S(1)}, bf16[48,1152]{1,0:T(8,128)(2,1)S(1)}, u32[]{:S(2)}, u32[]{:S(2)}) collective-permute-start(bf16[48,1152]{1,0:T(8,128)(2,1)S(1)} %collective-permute-done.1.refs_2_), channel_id=1, source_target_pairs={{0,32},{16,48},{32,64},{48,80},{64,96},{80,112},{96,128},{112,144}... | collective-permute-start | bytes 331784 | tf_op jit(solution)/shard_map/ppermute | solution.py:34
  43.1 3.9 %copy-start.1 = (bf16[256,1152]{1,0:T(8,128)(2,1)}, bf16[256,1152]{1,0:T(8,128)(2,1)S(1)}, u32[]{:S(2)}) copy-start(bf16[256,1152]{1,0:T(8,128)(2,1)S(1)} %shard_map.68.own_hbm) | copy-start | bytes 1769476
  43.1 3.9 %collective-permute-start.4 = (bf16[256,1152]{1,0:T(8,128)(2,1)S(1)}, bf16[256,1152]{1,0:T(8,128)(2,1)S(1)}, u32[]{:S(2)}, u32[]{:S(2)}) collective-permute-start(bf16[256,1152]{1,0:T(8,128)(2,1)S(1)} %shard_map.68.own_hbm), channel_id=1, source_target_pairs={{0,1},{1,0},{2,3},{3,2},{4,5},{5,4},{6,7},{7,6},{8,9},{9,8},{10,11... | collective-permute-start | bytes 1769480 | tf_op jit(solution)/shard_map/ppermute | solution.py:247
  47.0 0.8 copy-start.6
  47.0 1.4 %copy-start.5 = (bf16[16,48,1152]{2,1,0:T(8,128)(2,1)}, bf16[16,48,1152]{2,1,0:T(8,128)(2,1)S(1)}, u32[]{:S(2)}) copy-start(bf16[16,48,1152]{2,1,0:T(8,128)(2,1)S(1)} %all-to-all-done) | copy-start | bytes 5308420
  55.7 15.2 %copy-start = (f32[240,1280]{1,0:T(8,128)S(1)}, f32[240,1280]{1,0:T(8,128)}, u32[]{:S(2)}) copy-start(f32[240,1280]{1,0:T(8,128)} %get-tuple-element.17.ours_ref) | copy-start | bytes 3686404
  55.7 40.3 %all-to-all-start.1 = ((bf16[16,48,1152]{2,1,0:T(8,128)(2,1)}), bf16[16,48,1152]{2,1,0:T(8,128)(2,1)S(1)}, u32[]{:S(2)}, u32[]{:S(2)}) async-start(bf16[16,48,1152]{2,1,0:T(8,128)(2,1)} %bitcast.9), calls=%async_computation.1 | async-start | bytes 3538944 | tf_op jit(solution)/shard_map/all_to_all | solution.py:269
  66.6 22.8 %copy-start.2 = (bf16[48,1152]{1,0:T(8,128)(2,1)S(1)}, bf16[48,1152]{1,0:T(8,128)(2,1)}, u32[]{:S(2)}) copy-start(bf16[48,1152]{1,0:T(8,128)(2,1)} %image_ref.1) | copy-start | bytes 331780
  66.6 29.4 %copy-start.3 = (bf16[48,1152]{1,0:T(8,128)(2,1)S(1)}, bf16[48,1152]{1,0:T(8,128)(2,1)}, u32[]{:S(2)}) copy-start(bf16[48,1152]{1,0:T(8,128)(2,1)} %text_hbm.1) | copy-start | bytes 331780
  66.6 4.3 %collective-permute-start.5 = (bf16[240,1280]{1,0:T(8,128)(2,1)}, bf16[240,1280]{1,0:T(8,128)(2,1)S(1)}, u32[]{:S(2)}, u32[]{:S(2)}) collective-permute-start(bf16[240,1280]{1,0:T(8,128)(2,1)} %get-tuple-element.18), channel_id=1, source_target_pairs={{0,1},{1,0},{2,3},{3,2},{4,5},{5,4},{6,7},{7,6},{8,9},{9,8},{10,11... | collective-permute-start | bytes 1843208 | tf_op jit(solution)/shard_map/ppermute | solution.py:270
  71.1 8.6 %collective-permute-start.7 = (bf16[48,1280]{1,0:T(8,128)(2,1)S(1)}, bf16[48,1280]{1,0:T(8,128)(2,1)S(1)}, u32[]{:S(2)}, u32[]{:S(2)}) collective-permute-start(bf16[48,1280]{1,0:T(8,128)(2,1)S(1)} %get-tuple-element.22), channel_id=1, source_target_pairs={{0,992},{16,1008},{32,0},{48,16},{64,32},{80,48},{96,64},{112,80},... | collective-permute-start | bytes 368648 | tf_op jit(solution)/shard_map/ppermute | solution.py:34
  76.1 3.6 %collective-permute-start.8 = (bf16[48,1280]{1,0:T(8,128)(2,1)S(1)}, bf16[48,1280]{1,0:T(8,128)(2,1)S(1)}, u32[]{:S(2)}, u32[]{:S(2)}) collective-permute-start(bf16[48,1280]{1,0:T(8,128)(2,1)S(1)} %get-tuple-element.23), channel_id=1, source_target_pairs={{16,976},{48,1008},{80,16},{112,48},{144,80},{176,112},{208,144},{... | collective-permute-start | bytes 368648 | tf_op jit(solution)/shard_map/ppermute | solution.py:34
  76.8 7.2 %collective-permute-start.6 = (bf16[48,1280]{1,0:T(8,128)(2,1)S(1)}, bf16[48,1280]{1,0:T(8,128)(2,1)S(1)}, u32[]{:S(2)}, u32[]{:S(2)}) collective-permute-start(bf16[48,1280]{1,0:T(8,128)(2,1)S(1)} %get-tuple-element.20), channel_id=1, source_target_pairs={{0,992},{16,1008},{32,0},{48,16},{64,32},{80,48},{96,64},{112,80},... | collective-permute-start | bytes 368648 | tf_op jit(solution)/shard_map/ppermute | solution.py:34
  79.8 9.6 %collective-permute-start.9 = (bf16[48,1280]{1,0:T(8,128)(2,1)S(1)}, bf16[48,1280]{1,0:T(8,128)(2,1)S(1)}, u32[]{:S(2)}, u32[]{:S(2)}) collective-permute-start(bf16[48,1280]{1,0:T(8,128)(2,1)S(1)} %shard_map.71), channel_id=1, source_target_pairs={{0,960},{16,976},{32,992},{48,1008},{64,0},{80,16},{96,32},{112,48... | collective-permute-start | bytes 368648 | tf_op jit(solution)/shard_map/ppermute | solution.py:34
where the time goes:
time: 98.2 us; the launch traced here: 97.4 us
  starting transfers between devices  52.4 us (53%)
  waiting for transfers between devices  28.5 us (29%)
  Pallas kernels  12.4 us (13%)
  between operations  2.15 us (2%)
  local copies, waits for them, and re-layouts  1.4 us (1%)
    ppermute x8, starting transfers between devices, along_z(): return lax.ppermute(value, ('z', 'yl'), pairs)  20.8 us
    ppermute x8, waiting for transfers between devices, along_z(): return lax.ppermute(value, ('z', 'yl'), pairs)  20.4 us
    all_to_all x1, starting transfers between devices, per_device(): texts = lax.all_to_all(copies, PLANE, 0, 0, tiled=True)  16.8 us
    all_to_all x1, starting transfers between devices, per_device(): parts = lax.all_to_all(grads, PLANE, 0, 0, tiled=True)  10.9 us
    pallas_call x1, Pallas kernels, per_device(): call(functools.partial(score, rows), (gathered, jax.ShapeDtypeStruct(pack...  7.36 us
    all_to_all x1, waiting for transfers between devices, per_device(): parts = lax.all_to_all(grads, PLANE, 0, 0, tiled=True)  5.72 us
    pallas_call x1, Pallas kernels, per_device(): call(prepare, (gathered, low), in_specs=[hbm, hbm], out_specs=(hbm, hbm),...  2.42 us
    ppermute x1, waiting for transfers between devices, per_device(): lax.ppermute(theirs, 'core', swap)  2.22 us
  transfers between devices with their start and end apart: 12, of which 6 were waited for; matrix products, arithmetic and copies ran while one was open for 1% of the time, Pallas kernels for 1%

commit v1 on v0

--- a/solution.py
+++ b/solution.py
@@ -83,8 +83,8 @@
 
 
 def score(
-    rows, log_scale_ref, bias_ref, place_ref, text_hbm, own_hbm, other_hbm, grad_hbm, ours_hbm, theirs_hbm,
-    text_ref, image_ref, coef_ref, grad_ref, ours_ref, theirs_ref, in_sems, out_sems,
+    rows, scalars_hbm, text_hbm, own_hbm, other_hbm, grad_hbm, ours_hbm, theirs_hbm,
+    text_ref, image_ref, coef_ref, grad_ref, ours_ref, theirs_ref, scalars_ref, in_sems, out_sems, scalars_sem,
 ):
     half, width = text_hbm.shape
     piece = half // PIECES
@@ -99,14 +99,18 @@
     ]
     for fetch in image_fetches + text_fetches:
         fetch.start()
-    scale = jnp.exp(jnp.full((1, 1), log_scale_ref[0], jnp.float32))
-    parity, place = place_ref[0], place_ref[1]
+    scalars_fetch = pltpu.make_async_copy(scalars_hbm, scalars_ref, scalars_sem)
+    scalars_fetch.start()
+    parity, place = lax.axis_index("yl"), lax.axis_index(("x", "yh")) * rows
     cols = lax.broadcasted_iota(jnp.int32, (1, PACKED), 1)
     slot = jnp.zeros((1, PACKED), jnp.int32)
     for k in range(1, SLOTS):
         slot = slot + (cols >= k * rows).astype(jnp.int32)
     row_ids = lax.broadcasted_iota(jnp.int32, (piece, PACKED), 0)
     col_ids = lax.broadcasted_iota(jnp.int32, (piece, PACKED), 1)
+    scalars_fetch.wait()
+    scale = jnp.exp(scalars_ref[:1, :1])
+    bias = scalars_ref[8:9, :1]
     for fetch in image_fetches:
         fetch.wait()
 
@@ -132,7 +136,7 @@
             ahead = product(part + 1)
         for side in range(2):
             here = slice(side * PACKED, (side + 1) * PACKED)
-            logit = scale * now[:, here] + bias_ref[0]
+            logit = scale * now[:, here] + bias
             coef = 0.5 * jnp.tanh(0.5 * logit) + 0.5
             term = -jnp.log(1.0 - coef)
             if side == 0:
@@ -246,13 +250,13 @@
     own = call(pack, jax.ShapeDtypeStruct((PACKED, width), jnp.bfloat16))(image_low, one, two, three, four)
     other = lax.ppermute(own, "core", swap)
 
-    place = jnp.stack([lax.axis_index("yl"), lax.axis_index(("x", "yh")) * rows]).astype(jnp.int32)
+    scalars = jnp.concatenate([jnp.broadcast_to(value, (8, 128)) for value in (log_scale, bias)])
     packed = (SLOTS * rows, width + EXTRA)
     grads, ours, theirs = call(
         functools.partial(score, rows),
         (gathered, jax.ShapeDtypeStruct(packed, jnp.float32), jax.ShapeDtypeStruct(packed, jnp.bfloat16)),
         12 * half * PACKED * width,
-        in_specs=[smem] * 3 + [hbm] * 3,
+        in_specs=[hbm] * 4,
         out_specs=(hbm,) * 3,
         scratch_shapes=[
             pltpu.VMEM((half, width), jnp.bfloat16),
@@ -261,11 +265,13 @@
             pltpu.VMEM((half, width), jnp.bfloat16),
             pltpu.VMEM(packed, jnp.float32),
             pltpu.VMEM(packed, jnp.bfloat16),
+            pltpu.VMEM((16, 128), jnp.float32),
             dma((2 + PIECES,)),
             dma((2 + PIECES,)),
+            dma,
         ],
         limit=WHOLE,
-    )(log_scale, bias, place, texts, own, other)
+    )(scalars, texts, own, other)
     parts = lax.all_to_all(grads, PLANE, 0, 0, tiled=True)
     terms = call(join, (wide,) * SLOTS)(ours, lax.ppermute(theirs, "core", swap))
     middle = call(add, wide)(terms[2], along_z(terms[3], -1), along_z(terms[4], -2, (1,)))

time: 98.2 us -> 97.7 us (level); the launches traced: 97.4 us -> 95.9 us
  transfers between devices with their start and end apart: 12 -> 12, of which waited for: 6 -> 6; matrix products, arithmetic and copies ran while one was open for 1% -> 0% of each run, Pallas kernels for 1% -> 1%
where the time goes in v1:
time: 97.7 us; the launch traced here: 95.9 us
  starting transfers between devices  52.4 us (54%)
  waiting for transfers between devices  28.1 us (29%)
  Pallas kernels  11.8 us (12%)
  between operations  2.15 us (2%)
  local copies, waits for them, and re-layouts  1.44 us (1%)
    ppermute x8, starting transfers between devices, along_z(): return lax.ppermute(value, ('z', 'yl'), pairs)  20.8 us
    ppermute x8, waiting for transfers between devices, along_z(): return lax.ppermute(value, ('z', 'yl'), pairs)  20.5 us
    all_to_all x1, starting transfers between devices, per_device(): texts = lax.all_to_all(copies, PLANE, 0, 0, tiled=True)  16.8 us
    all_to_all x1, starting transfers between devices, per_device(): parts = lax.all_to_all(grads, PLANE, 0, 0, tiled=True)  10.9 us
    pallas_call x1, Pallas kernels, per_device(): call(functools.partial(score, rows), (gathered, jax.ShapeDtypeStruct(pack...  6.76 us
    all_to_all x1, waiting for transfers between devices, per_device(): parts = lax.all_to_all(grads, PLANE, 0, 0, tiled=True)  4.75 us
    pallas_call x1, Pallas kernels, per_device(): call(prepare, (gathered, low), in_specs=[hbm, hbm], out_specs=(hbm, hbm),...  2.42 us
    ppermute x1, waiting for transfers between devices, per_device(): lax.ppermute(theirs, 'core', swap)  2.22 us
  transfers between devices with their start and end apart: 12, of which 6 were waited for; matrix products, arithmetic and copies ran while one was open for 0% of the time, Pallas kernels for 1%

profile of v1, /device:TPU:6, one launch (start us, length us, event | category | flops | bytes accessed | tf_op | source)
XLA Modules:
  0.0 95.9 jit_solution(9345589420632948971)
XLA Ops:
  0.6 2.4 %shard_map.73 = (bf16[768,1152]{1,0:T(8,128)(2,1)}, bf16[48,1152]{1,0:T(8,128)(2,1)}) custom-call(bf16[48,1152]{1,0:T(8,128)(2,1)} %text_hbm.1, bf16[48,1152]{1,0:T(8,128)(2,1)} %image_ref.1), custom_call_target="tpu_custom_call" | custom-call | tf_op jit(solution)/shard_map/pallas_call | solution.py:237
  3.1 0.0 copy-start.4
  3.1 16.8 %all-to-all-start = ((bf16[16,48,1152]{2,1,0:T(8,128)(2,1)}), bf16[16,48,1152]{2,1,0:T(8,128)(2,1)S(1)}, u32[]{:S(2)}, u32[]{:S(2)}) async-start(bf16[16,48,1152]{2,1,0:T(8,128)(2,1)} %bitcast.11), calls=%async_computation | async-start | bytes 3538944 | tf_op jit(solution)/shard_map/all_to_all | solution.py:245
  19.9 0.0 copy-done.4
  19.9 1.9 %collective-permute-start.1 = (bf16[48,1152]{1,0:T(8,128)(2,1)S(1)}, bf16[48,1152]{1,0:T(8,128)(2,1)S(1)}, u32[]{:S(2)}, u32[]{:S(2)}) collective-permute-start(bf16[48,1152]{1,0:T(8,128)(2,1)S(1)} %copy-done.4), channel_id=1, source_target_pairs={{0,64},{16,80},{32,96},{48,112},{64,128},{80,144},{96,160},{112,17... | collective-permute-start | bytes 331784 | tf_op jit(solution)/shard_map/ppermute | solution.py:34
  21.8 1.9 %collective-permute-start = (bf16[48,1152]{1,0:T(8,128)(2,1)S(1)}, bf16[48,1152]{1,0:T(8,128)(2,1)S(1)}, u32[]{:S(2)}, u32[]{:S(2)}) collective-permute-start(bf16[48,1152]{1,0:T(8,128)(2,1)S(1)} %copy-done.4), channel_id=1, source_target_pairs={{0,32},{16,48},{32,64},{48,80},{64,96},{80,112},{96,128},{112,144}... | collective-permute-start | bytes 331784 | tf_op jit(solution)/shard_map/ppermute | solution.py:34
  23.7 10.8 %collective-permute-done.1.refs_2_ = bf16[48,1152]{1,0:T(8,128)(2,1)S(1)} collective-permute-done((bf16[48,1152]{1,0:T(8,128)(2,1)S(1)}, bf16[48,1152]{1,0:T(8,128)(2,1)S(1)}, u32[]{:S(2)}, u32[]{:S(2)}) %collective-permute-start.1) | collective-permute-done | bytes 110624 | tf_op jit(solution)/shard_map/ppermute | solution.py:34
  34.5 0.7 collective-permute-start.3
  35.2 3.6 %collective-permute-start.2 = (bf16[48,1152]{1,0:T(8,128)(2,1)S(1)}, bf16[48,1152]{1,0:T(8,128)(2,1)S(1)}, u32[]{:S(2)}, u32[]{:S(2)}) collective-permute-start(bf16[48,1152]{1,0:T(8,128)(2,1)S(1)} %collective-permute-done.1.refs_2_), channel_id=1, source_target_pairs={{0,32},{16,48},{32,64},{48,80},{64,96},{80,112},{96,128},{112,144}... | collective-permute-start | bytes 331784 | tf_op jit(solution)/shard_map/ppermute | solution.py:34
  38.8 0.0 collective-permute-done.refs_1_
  38.8 0.0 collective-permute-done.3.refs_4_
  38.8 4.2 %collective-permute-done.2.refs_3_ = bf16[48,1152]{1,0:T(8,128)(2,1)S(1)} collective-permute-done((bf16[48,1152]{1,0:T(8,128)(2,1)S(1)}, bf16[48,1152]{1,0:T(8,128)(2,1)S(1)}, u32[]{:S(2)}, u32[]{:S(2)}) %collective-permute-start.2) | collective-permute-done | bytes 110624 | tf_op jit(solution)/shard_map/ppermute | solution.py:34
  43.1 0.0 copy-start.1
  43.1 1.9 %collective-permute-start.4 = (bf16[256,1152]{1,0:T(8,128)(2,1)S(1)}, bf16[256,1152]{1,0:T(8,128)(2,1)S(1)}, u32[]{:S(2)}, u32[]{:S(2)}) collective-permute-start(bf16[256,1152]{1,0:T(8,128)(2,1)S(1)} %shard_map.74.own_hbm), channel_id=1, source_target_pairs={{0,1},{1,0},{2,3},{3,2},{4,5},{5,4},{6,7},{7,6},{8,9},{9,8},{10,11... | collective-permute-start | bytes 1769480 | tf_op jit(solution)/shard_map/ppermute | solution.py:251
  46.3 0.7 collective-permute-done.4.other_hbm
  47.0 0.0 copy-start.6
  47.0 0.0 all-to-all-done
  47.0 0.0 copy-start.5
  47.0 0.8 concatenate.6.scalars_hbm
  47.8 0.0 copy-done.1
  47.8 0.1 copy-done.6
  47.8 0.6 copy-done.5
  48.4 6.8 %shard_map.75 = (bf16[768,1152]{1,0:T(8,128)(2,1)}, f32[240,1280]{1,0:T(8,128)}, bf16[240,1280]{1,0:T(8,128)(2,1)}) custom-call(f32[16,128]{1,0:T(8,128)} %concatenate.6.scalars_hbm, bf16[768,1152]{1,0:T(8,128)(2,1)} %bitcast.10, bf16[256,1152]{1,0:T(8,128)(2,1)} %copy-done.1, bf16[256,1152]{1,0:T(8,128)(2,1)} %copy-done.6), custom_call_target="tpu_custom_call" | custom-call | flops 2717908992 | bytes 5308416 | tf_op jit(solution)/shard_map/pallas_call | solution.py:255
  55.2 0.0 copy-start
  55.2 10.9 %all-to-all-start.1 = ((bf16[16,48,1152]{2,1,0:T(8,128)(2,1)}), bf16[16,48,1152]{2,1,0:T(8,128)(2,1)S(1)}, u32[]{:S(2)}, u32[]{:S(2)}) async-start(bf16[16,48,1152]{2,1,0:T(8,128)(2,1)} %bitcast.9), calls=%async_computation.1 | async-start | bytes 3538944 | tf_op jit(solution)/shard_map/all_to_all | solution.py:275
  66.0 0.0 copy-start.2
  66.0 0.0 copy-start.3
  66.0 2.1 %collective-permute-start.5 = (bf16[240,1280]{1,0:T(8,128)(2,1)}, bf16[240,1280]{1,0:T(8,128)(2,1)S(1)}, u32[]{:S(2)}, u32[]{:S(2)}) collective-permute-start(bf16[240,1280]{1,0:T(8,128)(2,1)} %get-tuple-element.18), channel_id=1, source_target_pairs={{0,1},{1,0},{2,3},{3,2},{4,5},{5,4},{6,7},{7,6},{8,9},{9,8},{10,11... | collective-permute-start | bytes 1843208 | tf_op jit(solution)/shard_map/ppermute | solution.py:276
  68.1 2.2 %collective-permute-done.5.theirs_ref = bf16[240,1280]{1,0:T(8,128)(2,1)S(1)} collective-permute-done((bf16[240,1280]{1,0:T(8,128)(2,1)}, bf16[240,1280]{1,0:T(8,128)(2,1)S(1)}, u32[]{:S(2)}, u32[]{:S(2)}) %collective-permute-start.5) | collective-permute-done | bytes 614432 | tf_op jit(solution)/shard_map/ppermute | solution.py:276
  70.3 0.0 copy-done
  70.3 0.2 shard_map.76
  70.5 5.0 %collective-permute-start.7 = (bf16[48,1280]{1,0:T(8,128)(2,1)S(1)}, bf16[48,1280]{1,0:T(8,128)(2,1)S(1)}, u32[]{:S(2)}, u32[]{:S(2)}) collective-permute-start(bf16[48,1280]{1,0:T(8,128)(2,1)S(1)} %get-tuple-element.22), channel_id=1, source_target_pairs={{0,992},{16,1008},{32,0},{48,16},{64,32},{80,48},{96,64},{112,80},... | collective-permute-start | bytes 368648 | tf_op jit(solution)/shard_map/ppermute | solution.py:34
  75.5 0.7 collective-permute-start.8
  76.2 2.9 %collective-permute-start.6 = (bf16[48,1280]{1,0:T(8,128)(2,1)S(1)}, bf16[48,1280]{1,0:T(8,128)(2,1)S(1)}, u32[]{:S(2)}, u32[]{:S(2)}) collective-permute-start(bf16[48,1280]{1,0:T(8,128)(2,1)S(1)} %get-tuple-element.20), channel_id=1, source_target_pairs={{0,992},{16,1008},{32,0},{48,16},{64,32},{80,48},{96,64},{112,80},... | collective-permute-start | bytes 368648 | tf_op jit(solution)/shard_map/ppermute | solution.py:34
  79.1 0.0 collective-permute-done.7.refs_1_
  79.1 0.0 collective-permute-done.8.refs_2_
  79.1 0.1 shard_map.77
  79.3 4.1 %collective-permute-start.9 = (bf16[48,1280]{1,0:T(8,128)(2,1)S(1)}, bf16[48,1280]{1,0:T(8,128)(2,1)S(1)}, u32[]{:S(2)}, u32[]{:S(2)}) collective-permute-start(bf16[48,1280]{1,0:T(8,128)(2,1)S(1)} %shard_map.77), channel_id=1, source_target_pairs={{0,960},{16,976},{32,992},{48,1008},{64,0},{80,16},{96,32},{112,48... | collective-permute-start | bytes 368648 | tf_op jit(solution)/shard_map/ppermute | solution.py:34
  83.3 0.0 collective-permute-done.6.refs_1_
  83.3 5.5 %collective-permute-done.9.refs_2_ = bf16[48,1280]{1,0:T(8,128)(2,1)S(1)} collective-permute-done((bf16[48,1280]{1,0:T(8,128)(2,1)S(1)}, bf16[48,1280]{1,0:T(8,128)(2,1)S(1)}, u32[]{:S(2)}, u32[]{:S(2)}) %collective-permute-start.9) | collective-permute-done | bytes 122912 | tf_op jit(solution)/shard_map/ppermute | solution.py:34
  88.8 0.0 copy-done.2
  88.9 0.9 shard_map.78
  89.8 4.8 %all-to-all-done.1 = bf16[16,48,1152]{2,1,0:T(8,128)(2,1)S(1)} async-done(((bf16[16,48,1152]{2,1,0:T(8,128)(2,1)}), bf16[16,48,1152]{2,1,0:T(8,128)(2,1)S(1)}, u32[]{:S(2)}, u32[]{:S(2)}) %all-to-all-start.1) | async-done | bytes 1769504 | tf_op jit(solution)/shard_map/all_to_all | solution.py:275
  94.5 0.0 copy-done.3
  94.5 1.4 %shard_map.79 = f32[48,1152]{1,0:T(8,128)} custom-call(f32[1]{0:T(128)} %copy.7.log_scale_ref, bf16[48,1152]{1,0:T(8,128)(2,1)S(1)} %copy-done.3, bf16[768,1152]{1,0:T(8,128)(2,1)S(1)} %bitcast.8), custom_call_target="tpu_custom_call" | custom-call | tf_op jit(solution)/shard_map/pallas_call | solution.py:284
  (3 shorter events, 0.1 us)
Async XLA Ops:
  3.1 16.8 %copy-start.4 = (bf16[48,1152]{1,0:T(8,128)(2,1)S(1)}, bf16[48,1152]{1,0:T(8,128)(2,1)}, u32[]{:S(2)}) copy-start(bf16[48,1152]{1,0:T(8,128)(2,1)} %get-tuple-element.16.refs_0_) | copy-start | bytes 331780
  3.1 43.9 %all-to-all-start = ((bf16[16,48,1152]{2,1,0:T(8,128)(2,1)}), bf16[16,48,1152]{2,1,0:T(8,128)(2,1)S(1)}, u32[]{:S(2)}, u32[]{:S(2)}) async-start(bf16[16,48,1152]{2,1,0:T(8,128)(2,1)} %bitcast.11), calls=%async_computation | async-start | bytes 3538944 | tf_op jit(solution)/shard_map/all_to_all | solution.py:245
  19.9 14.6 %collective-permute-start.1 = (bf16[48,1152]{1,0:T(8,128)(2,1)S(1)}, bf16[48,1152]{1,0:T(8,128)(2,1)S(1)}, u32[]{:S(2)}, u32[]{:S(2)}) collective-permute-start(bf16[48,1152]{1,0:T(8,128)(2,1)S(1)} %copy-done.4), channel_id=1, source_target_pairs={{0,64},{16,80},{32,96},{48,112},{64,128},{80,144},{96,160},{112,17... | collective-permute-start | bytes 331784 | tf_op jit(solution)/shard_map/ppermute | solution.py:34
  21.8 17.0 %collective-permute-start = (bf16[48,1152]{1,0:T(8,128)(2,1)S(1)}, bf16[48,1152]{1,0:T(8,128)(2,1)S(1)}, u32[]{:S(2)}, u32[]{:S(2)}) collective-permute-start(bf16[48,1152]{1,0:T(8,128)(2,1)S(1)} %copy-done.4), channel_id=1, source_target_pairs={{0,32},{16,48},{32,64},{48,80},{64,96},{80,112},{96,128},{112,144}... | collective-permute-start | bytes 331784 | tf_op jit(solution)/shard_map/ppermute | solution.py:34
  34.5 4.3 %collective-permute-start.3 = (bf16[48,1152]{1,0:T(8,128)(2,1)S(1)}, bf16[48,1152]{1,0:T(8,128)(2,1)S(1)}, u32[]{:S(2)}, u32[]{:S(2)}) collective-permute-start(bf16[48,1152]{1,0:T(8,128)(2,1)S(1)} %collective-permute-done.1.refs_2_), channel_id=1, source_target_pairs={{16,80},{48,112},{80,144},{112,176},{144,208},{176,240},{208,272},... | collective-permute-start | bytes 331784 | tf_op jit(solution)/shard_map/ppermute | solution.py:34
  35.2 7.9 %collective-permute-start.2 = (bf16[48,1152]{1,0:T(8,128)(2,1)S(1)}, bf16[48,1152]{1,0:T(8,128)(2,1)S(1)}, u32[]{:S(2)}, u32[]{:S(2)}) collective-permute-start(bf16[48,1152]{1,0:T(8,128)(2,1)S(1)} %collective-permute-done.1.refs_2_), channel_id=1, source_target_pairs={{0,32},{16,48},{32,64},{48,80},{64,96},{80,112},{96,128},{112,144}... | collective-permute-start | bytes 331784 | tf_op jit(solution)/shard_map/ppermute | solution.py:34
  43.1 4.7 %copy-start.1 = (bf16[256,1152]{1,0:T(8,128)(2,1)}, bf16[256,1152]{1,0:T(8,128)(2,1)S(1)}, u32[]{:S(2)}) copy-start(bf16[256,1152]{1,0:T(8,128)(2,1)S(1)} %shard_map.74.own_hbm) | copy-start | bytes 1769476
  43.1 3.9 %collective-permute-start.4 = (bf16[256,1152]{1,0:T(8,128)(2,1)S(1)}, bf16[256,1152]{1,0:T(8,128)(2,1)S(1)}, u32[]{:S(2)}, u32[]{:S(2)}) collective-permute-start(bf16[256,1152]{1,0:T(8,128)(2,1)S(1)} %shard_map.74.own_hbm), channel_id=1, source_target_pairs={{0,1},{1,0},{2,3},{3,2},{4,5},{5,4},{6,7},{7,6},{8,9},{9,8},{10,11... | collective-permute-start | bytes 1769480 | tf_op jit(solution)/shard_map/ppermute | solution.py:251
  47.0 0.8 copy-start.6
  47.0 1.4 %copy-start.5 = (bf16[16,48,1152]{2,1,0:T(8,128)(2,1)}, bf16[16,48,1152]{2,1,0:T(8,128)(2,1)S(1)}, u32[]{:S(2)}) copy-start(bf16[16,48,1152]{2,1,0:T(8,128)(2,1)S(1)} %all-to-all-done) | copy-start | bytes 5308420
  55.2 15.2 %copy-start = (f32[240,1280]{1,0:T(8,128)S(1)}, f32[240,1280]{1,0:T(8,128)}, u32[]{:S(2)}) copy-start(f32[240,1280]{1,0:T(8,128)} %get-tuple-element.17.ours_ref) | copy-start | bytes 3686404
  55.2 39.3 %all-to-all-start.1 = ((bf16[16,48,1152]{2,1,0:T(8,128)(2,1)}), bf16[16,48,1152]{2,1,0:T(8,128)(2,1)S(1)}, u32[]{:S(2)}, u32[]{:S(2)}) async-start(bf16[16,48,1152]{2,1,0:T(8,128)(2,1)} %bitcast.9), calls=%async_computation.1 | async-start | bytes 3538944 | tf_op jit(solution)/shard_map/all_to_all | solution.py:275
  66.0 22.8 %copy-start.2 = (bf16[48,1152]{1,0:T(8,128)(2,1)S(1)}, bf16[48,1152]{1,0:T(8,128)(2,1)}, u32[]{:S(2)}) copy-start(bf16[48,1152]{1,0:T(8,128)(2,1)} %image_ref.1) | copy-start | bytes 331780
  66.0 28.5 %copy-start.3 = (bf16[48,1152]{1,0:T(8,128)(2,1)S(1)}, bf16[48,1152]{1,0:T(8,128)(2,1)}, u32[]{:S(2)}) copy-start(bf16[48,1152]{1,0:T(8,128)(2,1)} %text_hbm.1) | copy-start | bytes 331780
  66.0 4.3 %collective-permute-start.5 = (bf16[240,1280]{1,0:T(8,128)(2,1)}, bf16[240,1280]{1,0:T(8,128)(2,1)S(1)}, u32[]{:S(2)}, u32[]{:S(2)}) collective-permute-start(bf16[240,1280]{1,0:T(8,128)(2,1)} %get-tuple-element.18), channel_id=1, source_target_pairs={{0,1},{1,0},{2,3},{3,2},{4,5},{5,4},{6,7},{7,6},{8,9},{9,8},{10,11... | collective-permute-start | bytes 1843208 | tf_op jit(solution)/shard_map/ppermute | solution.py:276
  70.5 8.6 %collective-permute-start.7 = (bf16[48,1280]{1,0:T(8,128)(2,1)S(1)}, bf16[48,1280]{1,0:T(8,128)(2,1)S(1)}, u32[]{:S(2)}, u32[]{:S(2)}) collective-permute-start(bf16[48,1280]{1,0:T(8,128)(2,1)S(1)} %get-tuple-element.22), channel_id=1, source_target_pairs={{0,992},{16,1008},{32,0},{48,16},{64,32},{80,48},{96,64},{112,80},... | collective-permute-start | bytes 368648 | tf_op jit(solution)/shard_map/ppermute | solution.py:34
  75.5 3.6 %collective-permute-start.8 = (bf16[48,1280]{1,0:T(8,128)(2,1)S(1)}, bf16[48,1280]{1,0:T(8,128)(2,1)S(1)}, u32[]{:S(2)}, u32[]{:S(2)}) collective-permute-start(bf16[48,1280]{1,0:T(8,128)(2,1)S(1)} %get-tuple-element.23), channel_id=1, source_target_pairs={{16,976},{48,1008},{80,16},{112,48},{144,80},{176,112},{208,144},{... | collective-permute-start | bytes 368648 | tf_op jit(solution)/shard_map/ppermute | solution.py:34
  76.2 7.2 %collective-permute-start.6 = (bf16[48,1280]{1,0:T(8,128)(2,1)S(1)}, bf16[48,1280]{1,0:T(8,128)(2,1)S(1)}, u32[]{:S(2)}, u32[]{:S(2)}) collective-permute-start(bf16[48,1280]{1,0:T(8,128)(2,1)S(1)} %get-tuple-element.20), channel_id=1, source_target_pairs={{0,992},{16,1008},{32,0},{48,16},{64,32},{80,48},{96,64},{112,80},... | collective-permute-start | bytes 368648 | tf_op jit(solution)/shard_map/ppermute | solution.py:34
  79.3 9.6 %collective-permute-start.9 = (bf16[48,1280]{1,0:T(8,128)(2,1)S(1)}, bf16[48,1280]{1,0:T(8,128)(2,1)S(1)}, u32[]{:S(2)}, u32[]{:S(2)}) collective-permute-start(bf16[48,1280]{1,0:T(8,128)(2,1)S(1)} %shard_map.77), channel_id=1, source_target_pairs={{0,960},{16,976},{32,992},{48,1008},{64,0},{80,16},{96,32},{112,48... | collective-permute-start | bytes 368648 | tf_op jit(solution)/shard_map/ppermute | solution.py:34

commit v2 on v1

--- a/solution.py
+++ b/solution.py
@@ -97,7 +97,7 @@
         pltpu.make_async_copy(text_hbm.at[span], text_ref.at[span], in_sems.at[2 + part])
         for part, span in enumerate(spans)
     ]
-    for fetch in image_fetches + text_fetches:
+    for fetch in text_fetches[:1] + image_fetches + text_fetches[1:]:
         fetch.start()
     scalars_fetch = pltpu.make_async_copy(scalars_hbm, scalars_ref, scalars_sem)
     scalars_fetch.start()
@@ -176,7 +176,7 @@
     rows = grad_refs[0].shape[0]
     for k, grad_ref in enumerate(grad_refs):
         here = slice(k * rows, (k + 1) * rows)
-        store_sum(grad_ref, ours_ref[here, :] + theirs_ref[here, :].astype(jnp.float32))
+        store_sum(grad_ref, ours_ref[here, :].astype(jnp.float32) + theirs_ref[here, :].astype(jnp.float32))
 
 
 def sum_of(refs):
@@ -254,7 +254,7 @@
     packed = (SLOTS * rows, width + EXTRA)
     grads, ours, theirs = call(
         functools.partial(score, rows),
-        (gathered, jax.ShapeDtypeStruct(packed, jnp.float32), jax.ShapeDtypeStruct(packed, jnp.bfloat16)),
+        (gathered, jax.ShapeDtypeStruct(packed, jnp.bfloat16), jax.ShapeDtypeStruct(packed, jnp.bfloat16)),
         12 * half * PACKED * width,
         in_specs=[hbm] * 4,
         out_specs=(hbm,) * 3,
@@ -263,7 +263,7 @@
             pltpu.VMEM((2 * PACKED, width), jnp.bfloat16),
             pltpu.VMEM((half, 2 * PACKED), jnp.bfloat16),
             pltpu.VMEM((half, width), jnp.bfloat16),
-            pltpu.VMEM(packed, jnp.float32),
+            pltpu.VMEM(packed, jnp.bfloat16),
             pltpu.VMEM(packed, jnp.bfloat16),
             pltpu.VMEM((16, 128), jnp.float32),
             dma((2 + PIECES,)),

time: 97.7 us -> 97.3 us (level)
  no operation moved by 1% of the time
where the time goes in v2:
time: 97.3 us; the launch traced here: 95.7 us
  starting transfers between devices  52.4 us (54%)
  waiting for transfers between devices  28.1 us (29%)
  Pallas kernels  11.6 us (12%)
  between operations  2.17 us (2%)
  local copies, waits for them, and re-layouts  1.45 us (1%)
    ppermute x8, starting transfers between devices, along_z(): return lax.ppermute(value, ('z', 'yl'), pairs)  20.8 us
    ppermute x8, waiting for transfers between devices, along_z(): return lax.ppermute(value, ('z', 'yl'), pairs)  20.4 us
    all_to_all x1, starting transfers between devices, per_device(): texts = lax.all_to_all(copies, PLANE, 0, 0, tiled=True)  16.8 us
    all_to_all x1, starting transfers between devices, per_device(): parts = lax.all_to_all(grads, PLANE, 0, 0, tiled=True)  10.9 us
    pallas_call x1, Pallas kernels, per_device(): call(functools.partial(score, rows), (gathered, jax.ShapeDtypeStruct(pack...  6.56 us
    all_to_all x1, waiting for transfers between devices, per_device(): parts = lax.all_to_all(grads, PLANE, 0, 0, tiled=True)  4.95 us
    pallas_call x1, Pallas kernels, per_device(): call(prepare, (gathered, low), in_specs=[hbm, hbm], out_specs=(hbm, hbm),...  2.43 us
    ppermute x1, starting transfers between devices, per_device(): lax.ppermute(theirs, 'core', swap)  2.05 us
  transfers between devices with their start and end apart: 12, of which 6 were waited for; matrix products, arithmetic and copies ran while one was open for 0% of the time, Pallas kernels for 1%

profile of v2, /device:TPU:6, one launch (start us, length us, event | category | flops | bytes accessed | tf_op | source)
XLA Modules:
  0.0 95.7 jit_solution(12189214575813075963)
XLA Ops:
  0.6 2.4 %shard_map.73 = (bf16[768,1152]{1,0:T(8,128)(2,1)}, bf16[48,1152]{1,0:T(8,128)(2,1)}) custom-call(bf16[48,1152]{1,0:T(8,128)(2,1)} %text_hbm.1, bf16[48,1152]{1,0:T(8,128)(2,1)} %image_ref.1), custom_call_target="tpu_custom_call" | custom-call | tf_op jit(solution)/shard_map/pallas_call | solution.py:237
  3.1 0.0 copy-start.4
  3.1 16.8 %all-to-all-start = ((bf16[16,48,1152]{2,1,0:T(8,128)(2,1)}), bf16[16,48,1152]{2,1,0:T(8,128)(2,1)S(1)}, u32[]{:S(2)}, u32[]{:S(2)}) async-start(bf16[16,48,1152]{2,1,0:T(8,128)(2,1)} %bitcast.11), calls=%async_computation | async-start | bytes 3538944 | tf_op jit(solution)/shard_map/all_to_all | solution.py:245
  19.9 0.0 copy-done.4
  19.9 1.9 %collective-permute-start.1 = (bf16[48,1152]{1,0:T(8,128)(2,1)S(1)}, bf16[48,1152]{1,0:T(8,128)(2,1)S(1)}, u32[]{:S(2)}, u32[]{:S(2)}) collective-permute-start(bf16[48,1152]{1,0:T(8,128)(2,1)S(1)} %copy-done.4), channel_id=1, source_target_pairs={{0,64},{16,80},{32,96},{48,112},{64,128},{80,144},{96,160},{112,17... | collective-permute-start | bytes 331784 | tf_op jit(solution)/shard_map/ppermute | solution.py:34
  21.8 1.9 %collective-permute-start = (bf16[48,1152]{1,0:T(8,128)(2,1)S(1)}, bf16[48,1152]{1,0:T(8,128)(2,1)S(1)}, u32[]{:S(2)}, u32[]{:S(2)}) collective-permute-start(bf16[48,1152]{1,0:T(8,128)(2,1)S(1)} %copy-done.4), channel_id=1, source_target_pairs={{0,32},{16,48},{32,64},{48,80},{64,96},{80,112},{96,128},{112,144}... | collective-permute-start | bytes 331784 | tf_op jit(solution)/shard_map/ppermute | solution.py:34
  23.7 10.8 %collective-permute-done.1.refs_2_ = bf16[48,1152]{1,0:T(8,128)(2,1)S(1)} collective-permute-done((bf16[48,1152]{1,0:T(8,128)(2,1)S(1)}, bf16[48,1152]{1,0:T(8,128)(2,1)S(1)}, u32[]{:S(2)}, u32[]{:S(2)}) %collective-permute-start.1) | collective-permute-done | bytes 110624 | tf_op jit(solution)/shard_map/ppermute | solution.py:34
  34.5 0.7 collective-permute-start.3
  35.2 3.6 %collective-permute-start.2 = (bf16[48,1152]{1,0:T(8,128)(2,1)S(1)}, bf16[48,1152]{1,0:T(8,128)(2,1)S(1)}, u32[]{:S(2)}, u32[]{:S(2)}) collective-permute-start(bf16[48,1152]{1,0:T(8,128)(2,1)S(1)} %collective-permute-done.1.refs_2_), channel_id=1, source_target_pairs={{0,32},{16,48},{32,64},{48,80},{64,96},{80,112},{96,128},{112,144}... | collective-permute-start | bytes 331784 | tf_op jit(solution)/shard_map/ppermute | solution.py:34
  38.8 0.0 collective-permute-done.refs_1_
  38.8 0.0 collective-permute-done.3.refs_4_
  38.9 4.2 %collective-permute-done.2.refs_3_ = bf16[48,1152]{1,0:T(8,128)(2,1)S(1)} collective-permute-done((bf16[48,1152]{1,0:T(8,128)(2,1)S(1)}, bf16[48,1152]{1,0:T(8,128)(2,1)S(1)}, u32[]{:S(2)}, u32[]{:S(2)}) %collective-permute-start.2) | collective-permute-done | bytes 110624 | tf_op jit(solution)/shard_map/ppermute | solution.py:34
  43.1 0.0 copy-start.1
  43.1 1.9 %collective-permute-start.4 = (bf16[256,1152]{1,0:T(8,128)(2,1)S(1)}, bf16[256,1152]{1,0:T(8,128)(2,1)S(1)}, u32[]{:S(2)}, u32[]{:S(2)}) collective-permute-start(bf16[256,1152]{1,0:T(8,128)(2,1)S(1)} %shard_map.74.own_hbm), channel_id=1, source_target_pairs={{0,1},{1,0},{2,3},{3,2},{4,5},{5,4},{6,7},{7,6},{8,9},{9,8},{10,11... | collective-permute-start | bytes 1769480 | tf_op jit(solution)/shard_map/ppermute | solution.py:251
  46.3 0.7 collective-permute-done.4.other_hbm
  47.0 0.0 copy-start.7
  47.0 0.0 all-to-all-done
  47.0 0.0 copy-start.5
  47.0 0.8 concatenate.6.scalars_hbm
  47.8 0.0 copy-done.1
  47.8 0.0 copy-done.7
  47.8 0.6 copy-done.5
  48.4 6.6 %shard_map.75 = (bf16[768,1152]{1,0:T(8,128)(2,1)}, bf16[240,1280]{1,0:T(8,128)(2,1)}, bf16[240,1280]{1,0:T(8,128)(2,1)}) custom-call(f32[16,128]{1,0:T(8,128)} %concatenate.6.scalars_hbm, bf16[768,1152]{1,0:T(8,128)(2,1)} %bitcast.10, bf16[256,1152]{1,0:T(8,128)(2,1)} %copy-done.1, bf16[256,1152]{1,0:T(8,128)(2,1)} %copy-done.7), custom_call_target="tpu_custom_call" | custom-call | flops 2717908992 | bytes 5308416 | tf_op jit(solution)/shard_map/pallas_call | solution.py:255
  55.0 0.0 copy-start.6
  55.0 0.0 copy-start
  55.0 0.0 copy-start.2
  55.0 10.9 %all-to-all-start.1 = ((bf16[16,48,1152]{2,1,0:T(8,128)(2,1)}), bf16[16,48,1152]{2,1,0:T(8,128)(2,1)S(1)}, u32[]{:S(2)}, u32[]{:S(2)}) async-start(bf16[16,48,1152]{2,1,0:T(8,128)(2,1)} %bitcast.9), calls=%async_computation.1 | async-start | bytes 3538944 | tf_op jit(solution)/shard_map/all_to_all | solution.py:275
  65.9 0.0 copy-start.3
  65.9 0.0 copy-done.6
  65.9 2.1 %collective-permute-start.5 = (bf16[240,1280]{1,0:T(8,128)(2,1)S(1)}, bf16[240,1280]{1,0:T(8,128)(2,1)S(1)}, u32[]{:S(2)}, u32[]{:S(2)}) collective-permute-start(bf16[240,1280]{1,0:T(8,128)(2,1)S(1)} %copy-done.6), channel_id=1, source_target_pairs={{0,1},{1,0},{2,3},{3,2},{4,5},{5,4},{6,7},{7,6},{8,9},{9,8},{10,11... | collective-permute-start | bytes 1843208 | tf_op jit(solution)/shard_map/ppermute | solution.py:276
  67.9 2.0 %collective-permute-done.5.theirs_ref = bf16[240,1280]{1,0:T(8,128)(2,1)S(1)} collective-permute-done((bf16[240,1280]{1,0:T(8,128)(2,1)S(1)}, bf16[240,1280]{1,0:T(8,128)(2,1)S(1)}, u32[]{:S(2)}, u32[]{:S(2)}) %collective-permute-start.5) | collective-permute-done | bytes 614432 | tf_op jit(solution)/shard_map/ppermute | solution.py:276
  69.9 0.0 copy-done
  69.9 0.2 shard_map.76
  70.2 5.0 %collective-permute-start.7 = (bf16[48,1280]{1,0:T(8,128)(2,1)S(1)}, bf16[48,1280]{1,0:T(8,128)(2,1)S(1)}, u32[]{:S(2)}, u32[]{:S(2)}) collective-permute-start(bf16[48,1280]{1,0:T(8,128)(2,1)S(1)} %get-tuple-element.22), channel_id=1, source_target_pairs={{0,992},{16,1008},{32,0},{48,16},{64,32},{80,48},{96,64},{112,80},... | collective-permute-start | bytes 368648 | tf_op jit(solution)/shard_map/ppermute | solution.py:34
  75.2 0.7 collective-permute-start.8
  75.8 2.9 %collective-permute-start.6 = (bf16[48,1280]{1,0:T(8,128)(2,1)S(1)}, bf16[48,1280]{1,0:T(8,128)(2,1)S(1)}, u32[]{:S(2)}, u32[]{:S(2)}) collective-permute-start(bf16[48,1280]{1,0:T(8,128)(2,1)S(1)} %get-tuple-element.20), channel_id=1, source_target_pairs={{0,992},{16,1008},{32,0},{48,16},{64,32},{80,48},{96,64},{112,80},... | collective-permute-start | bytes 368648 | tf_op jit(solution)/shard_map/ppermute | solution.py:34
  78.8 0.0 collective-permute-done.7.refs_1_
  78.8 0.0 collective-permute-done.8.refs_2_
  78.8 0.1 shard_map.77
  78.9 4.1 %collective-permute-start.9 = (bf16[48,1280]{1,0:T(8,128)(2,1)S(1)}, bf16[48,1280]{1,0:T(8,128)(2,1)S(1)}, u32[]{:S(2)}, u32[]{:S(2)}) collective-permute-start(bf16[48,1280]{1,0:T(8,128)(2,1)S(1)} %shard_map.77), channel_id=1, source_target_pairs={{0,960},{16,976},{32,992},{48,1008},{64,0},{80,16},{96,32},{112,48... | collective-permute-start | bytes 368648 | tf_op jit(solution)/shard_map/ppermute | solution.py:34
  83.0 0.0 collective-permute-done.6.refs_1_
  83.0 5.5 %collective-permute-done.9.refs_2_ = bf16[48,1280]{1,0:T(8,128)(2,1)S(1)} collective-permute-done((bf16[48,1280]{1,0:T(8,128)(2,1)S(1)}, bf16[48,1280]{1,0:T(8,128)(2,1)S(1)}, u32[]{:S(2)}, u32[]{:S(2)}) %collective-permute-start.9) | collective-permute-done | bytes 122912 | tf_op jit(solution)/shard_map/ppermute | solution.py:34
  88.5 0.0 copy-done.2
  88.5 0.9 shard_map.78
  89.4 5.0 %all-to-all-done.1 = bf16[16,48,1152]{2,1,0:T(8,128)(2,1)S(1)} async-done(((bf16[16,48,1152]{2,1,0:T(8,128)(2,1)}), bf16[16,48,1152]{2,1,0:T(8,128)(2,1)S(1)}, u32[]{:S(2)}, u32[]{:S(2)}) %all-to-all-start.1) | async-done | bytes 1769504 | tf_op jit(solution)/shard_map/all_to_all | solution.py:275
  94.4 0.0 copy-done.3
  94.4 1.4 %shard_map.79 = f32[48,1152]{1,0:T(8,128)} custom-call(f32[1]{0:T(128)} %copy.7.log_scale_ref, bf16[48,1152]{1,0:T(8,128)(2,1)S(1)} %copy-done.3, bf16[768,1152]{1,0:T(8,128)(2,1)S(1)} %bitcast.8), custom_call_target="tpu_custom_call" | custom-call | tf_op jit(solution)/shard_map/pallas_call | solution.py:284
  (3 shorter events, 0.1 us)
Async XLA Ops:
  3.1 16.8 %copy-start.4 = (bf16[48,1152]{1,0:T(8,128)(2,1)S(1)}, bf16[48,1152]{1,0:T(8,128)(2,1)}, u32[]{:S(2)}) copy-start(bf16[48,1152]{1,0:T(8,128)(2,1)} %get-tuple-element.16.refs_0_) | copy-start | bytes 331780
  3.1 43.9 %all-to-all-start = ((bf16[16,48,1152]{2,1,0:T(8,128)(2,1)}), bf16[16,48,1152]{2,1,0:T(8,128)(2,1)S(1)}, u32[]{:S(2)}, u32[]{:S(2)}) async-start(bf16[16,48,1152]{2,1,0:T(8,128)(2,1)} %bitcast.11), calls=%async_computation | async-start | bytes 3538944 | tf_op jit(solution)/shard_map/all_to_all | solution.py:245
  19.9 14.6 %collective-permute-start.1 = (bf16[48,1152]{1,0:T(8,128)(2,1)S(1)}, bf16[48,1152]{1,0:T(8,128)(2,1)S(1)}, u32[]{:S(2)}, u32[]{:S(2)}) collective-permute-start(bf16[48,1152]{1,0:T(8,128)(2,1)S(1)} %copy-done.4), channel_id=1, source_target_pairs={{0,64},{16,80},{32,96},{48,112},{64,128},{80,144},{96,160},{112,17... | collective-permute-start | bytes 331784 | tf_op jit(solution)/shard_map/ppermute | solution.py:34
  21.8 17.0 %collective-permute-start = (bf16[48,1152]{1,0:T(8,128)(2,1)S(1)}, bf16[48,1152]{1,0:T(8,128)(2,1)S(1)}, u32[]{:S(2)}, u32[]{:S(2)}) collective-permute-start(bf16[48,1152]{1,0:T(8,128)(2,1)S(1)} %copy-done.4), channel_id=1, source_target_pairs={{0,32},{16,48},{32,64},{48,80},{64,96},{80,112},{96,128},{112,144}... | collective-permute-start | bytes 331784 | tf_op jit(solution)/shard_map/ppermute | solution.py:34
  34.5 4.3 %collective-permute-start.3 = (bf16[48,1152]{1,0:T(8,128)(2,1)S(1)}, bf16[48,1152]{1,0:T(8,128)(2,1)S(1)}, u32[]{:S(2)}, u32[]{:S(2)}) collective-permute-start(bf16[48,1152]{1,0:T(8,128)(2,1)S(1)} %collective-permute-done.1.refs_2_), channel_id=1, source_target_pairs={{16,80},{48,112},{80,144},{112,176},{144,208},{176,240},{208,272},... | collective-permute-start | bytes 331784 | tf_op jit(solution)/shard_map/ppermute | solution.py:34
  35.2 7.9 %collective-permute-start.2 = (bf16[48,1152]{1,0:T(8,128)(2,1)S(1)}, bf16[48,1152]{1,0:T(8,128)(2,1)S(1)}, u32[]{:S(2)}, u32[]{:S(2)}) collective-permute-start(bf16[48,1152]{1,0:T(8,128)(2,1)S(1)} %collective-permute-done.1.refs_2_), channel_id=1, source_target_pairs={{0,32},{16,48},{32,64},{48,80},{64,96},{80,112},{96,128},{112,144}... | collective-permute-start | bytes 331784 | tf_op jit(solution)/shard_map/ppermute | solution.py:34
  43.1 4.7 %copy-start.1 = (bf16[256,1152]{1,0:T(8,128)(2,1)}, bf16[256,1152]{1,0:T(8,128)(2,1)S(1)}, u32[]{:S(2)}) copy-start(bf16[256,1152]{1,0:T(8,128)(2,1)S(1)} %shard_map.74.own_hbm) | copy-start | bytes 1769476
  43.1 3.9 %collective-permute-start.4 = (bf16[256,1152]{1,0:T(8,128)(2,1)S(1)}, bf16[256,1152]{1,0:T(8,128)(2,1)S(1)}, u32[]{:S(2)}, u32[]{:S(2)}) collective-permute-start(bf16[256,1152]{1,0:T(8,128)(2,1)S(1)} %shard_map.74.own_hbm), channel_id=1, source_target_pairs={{0,1},{1,0},{2,3},{3,2},{4,5},{5,4},{6,7},{7,6},{8,9},{9,8},{10,11... | collective-permute-start | bytes 1769480 | tf_op jit(solution)/shard_map/ppermute | solution.py:251
  47.0 0.8 copy-start.7
  47.0 1.4 %copy-start.5 = (bf16[16,48,1152]{2,1,0:T(8,128)(2,1)}, bf16[16,48,1152]{2,1,0:T(8,128)(2,1)S(1)}, u32[]{:S(2)}) copy-start(bf16[16,48,1152]{2,1,0:T(8,128)(2,1)S(1)} %all-to-all-done) | copy-start | bytes 5308420
  55.0 10.9 %copy-start.6 = (bf16[240,1280]{1,0:T(8,128)(2,1)S(1)}, bf16[240,1280]{1,0:T(8,128)(2,1)}, u32[]{:S(2)}) copy-start(bf16[240,1280]{1,0:T(8,128)(2,1)} %get-tuple-element.18) | copy-start | bytes 1843204
  55.0 15.0 %copy-start = (bf16[240,1280]{1,0:T(8,128)(2,1)S(1)}, bf16[240,1280]{1,0:T(8,128)(2,1)}, u32[]{:S(2)}) copy-start(bf16[240,1280]{1,0:T(8,128)(2,1)} %get-tuple-element.17.ours_ref) | copy-start | bytes 1843204
  55.0 33.5 %copy-start.2 = (bf16[48,1152]{1,0:T(8,128)(2,1)S(1)}, bf16[48,1152]{1,0:T(8,128)(2,1)}, u32[]{:S(2)}) copy-start(bf16[48,1152]{1,0:T(8,128)(2,1)} %image_ref.1) | copy-start | bytes 331780
  55.0 39.3 %all-to-all-start.1 = ((bf16[16,48,1152]{2,1,0:T(8,128)(2,1)}), bf16[16,48,1152]{2,1,0:T(8,128)(2,1)S(1)}, u32[]{:S(2)}, u32[]{:S(2)}) async-start(bf16[16,48,1152]{2,1,0:T(8,128)(2,1)} %bitcast.9), calls=%async_computation.1 | async-start | bytes 3538944 | tf_op jit(solution)/shard_map/all_to_all | solution.py:275
  65.9 28.5 %copy-start.3 = (bf16[48,1152]{1,0:T(8,128)(2,1)S(1)}, bf16[48,1152]{1,0:T(8,128)(2,1)}, u32[]{:S(2)}) copy-start(bf16[48,1152]{1,0:T(8,128)(2,1)} %text_hbm.1) | copy-start | bytes 331780
  65.9 4.1 %collective-permute-start.5 = (bf16[240,1280]{1,0:T(8,128)(2,1)S(1)}, bf16[240,1280]{1,0:T(8,128)(2,1)S(1)}, u32[]{:S(2)}, u32[]{:S(2)}) collective-permute-start(bf16[240,1280]{1,0:T(8,128)(2,1)S(1)} %copy-done.6), channel_id=1, source_target_pairs={{0,1},{1,0},{2,3},{3,2},{4,5},{5,4},{6,7},{7,6},{8,9},{9,8},{10,11... | collective-permute-start | bytes 1843208 | tf_op jit(solution)/shard_map/ppermute | solution.py:276
  70.2 8.6 %collective-permute-start.7 = (bf16[48,1280]{1,0:T(8,128)(2,1)S(1)}, bf16[48,1280]{1,0:T(8,128)(2,1)S(1)}, u32[]{:S(2)}, u32[]{:S(2)}) collective-permute-start(bf16[48,1280]{1,0:T(8,128)(2,1)S(1)} %get-tuple-element.22), channel_id=1, source_target_pairs={{0,992},{16,1008},{32,0},{48,16},{64,32},{80,48},{96,64},{112,80},... | collective-permute-start | bytes 368648 | tf_op jit(solution)/shard_map/ppermute | solution.py:34
  75.2 3.6 %collective-permute-start.8 = (bf16[48,1280]{1,0:T(8,128)(2,1)S(1)}, bf16[48,1280]{1,0:T(8,128)(2,1)S(1)}, u32[]{:S(2)}, u32[]{:S(2)}) collective-permute-start(bf16[48,1280]{1,0:T(8,128)(2,1)S(1)} %get-tuple-element.23), channel_id=1, source_target_pairs={{16,976},{48,1008},{80,16},{112,48},{144,80},{176,112},{208,144},{... | collective-permute-start | bytes 368648 | tf_op jit(solution)/shard_map/ppermute | solution.py:34
  75.8 7.2 %collective-permute-start.6 = (bf16[48,1280]{1,0:T(8,128)(2,1)S(1)}, bf16[48,1280]{1,0:T(8,128)(2,1)S(1)}, u32[]{:S(2)}, u32[]{:S(2)}) collective-permute-start(bf16[48,1280]{1,0:T(8,128)(2,1)S(1)} %get-tuple-element.20), channel_id=1, source_target_pairs={{0,992},{16,1008},{32,0},{48,16},{64,32},{80,48},{96,64},{112,80},... | collective-permute-start | bytes 368648 | tf_op jit(solution)/shard_map/ppermute | solution.py:34
  78.9 9.6 %collective-permute-start.9 = (bf16[48,1280]{1,0:T(8,128)(2,1)S(1)}, bf16[48,1280]{1,0:T(8,128)(2,1)S(1)}, u32[]{:S(2)}, u32[]{:S(2)}) collective-permute-start(bf16[48,1280]{1,0:T(8,128)(2,1)S(1)} %shard_map.77), channel_id=1, source_target_pairs={{0,960},{16,976},{32,992},{48,1008},{64,0},{80,16},{96,32},{112,48... | collective-permute-start | bytes 368648 | tf_op jit(solution)/shard_map/ppermute | solution.py:34
